TPU v7x, 512 devices: a whole 4x4x16 slice. The times are simulated.
512 devices in a mesh: dp: 64 (over z, x), crop: 2 (over core), proto: 4 (over y).
Axes of the slice: x: 4, y: 4, z: 16, core: 2. Of those that a mesh axis runs over, the one named last changes fastest.
Arguments:
- features: bfloat16 [2, 3072, 256], P('crop', 'dp'), may hold values from -6 to 6
- targets: bfloat16 [3072, 131072], P('crop', ('dp', 'proto')), may hold values from 9.968062e-10 to 9.9658966e-05
- partner: int32 [2, 192], P('crop'), may hold values from 0 to 191
- vectors: float32 [131072, 256], P(('dp', 'proto', 'crop')), may hold values from -0.375 to 0.375
- first: float32 [131072, 256], P(('dp', 'proto', 'crop')), may hold values from -0.0014648438 to 0.0014648438
- second: float32 [131072, 256], P(('dp', 'proto', 'crop')), may hold values from 1e-08 to 1e-07
- teacher: float32 [131072, 256], P(('dp', 'proto', 'crop')), may hold values from -0.375 to 0.375
Outputs:
- grad_features: float32 [2, 3072, 256], P('crop', 'dp')
- new_vectors: float32 [131072, 256], P(('dp', 'proto', 'crop'))
- new_first: float32 [131072, 256], P(('dp', 'proto', 'crop'))
- new_second: float32 [131072, 256], P(('dp', 'proto', 'crop'))
- new_teacher: float32 [131072, 256], P(('dp', 'proto', 'crop'))
All inputs are finite; a program needn't handle non-finite values.
Results may differ from a plain program's by a relative error of at most 0.004.
The roundings to bfloat16 on the way count: a program that leaves them out, or rounds other values in their place, can miss the bound.
Values may be sent and summed in bfloat16 or wider, within the bound.
No kernel may reach another device: no remote copies, remote signals or barrier semaphores. Data moves between devices by JAX's collectives and lax.ppermute only.
A program may use at most 64 MiB of HBM per device.

v0:
```python
import functools

import jax
import jax.numpy as jnp
from jax import lax
from jax.experimental import pallas as pl
from jax.experimental.pallas import tpu as pltpu
from jax.sharding import Mesh, PartitionSpec as P

TILE = 16
AXES = ("z", "x", "crop", "y")
PLANE = ("x", "y")
LANES = 128
BLOCK = 768


student_temp = 0.1
norm_eps = 1e-06
learn_rate = 0.01
weight_decay = 0.04
beta_first = 0.9
beta_second = 0.999
bias_first = 0.9999734386011124
bias_second = 0.0952078536
adam_eps = 1e-08
teacher_keep = 0.996


def swapped(shard):
    return lax.ppermute(shard, "crop", [(0, 1), (1, 0)])


def exchanged(blocks, axes):
    return lax.all_to_all(blocks, axes, 0, 0, tiled=True)


def norm_back(upstream, feats):
    length = jnp.sqrt(jnp.sum(feats * feats, 1, keepdims=True) + norm_eps)
    unit = feats / length
    return (upstream - unit * jnp.sum(unit * upstream, 1, keepdims=True)) / length


def adamw_rows(grad_rows, vectors, first, second, teacher):
    vlen = jnp.sqrt(jnp.sum(vectors * vectors, 1, keepdims=True) + norm_eps)
    unit = vectors / vlen
    dvec = (grad_rows - unit * jnp.sum(unit * grad_rows, 1, keepdims=True)) / vlen
    new_first = beta_first * first + (1.0 - beta_first) * dvec
    new_second = beta_second * second + (1.0 - beta_second) * dvec * dvec
    update = (
        new_first / bias_first / (jnp.sqrt(new_second / bias_second) + adam_eps)
        + weight_decay * vectors
    )
    new_vectors = vectors - learn_rate * update
    new_teacher = teacher_keep * teacher + (1.0 - teacher_keep) * new_vectors
    return (new_vectors, new_first, new_second, new_teacher)


def row_sums(block):
    folded = block[:, :LANES]
    for start in range(LANES, block.shape[1], LANES):
        folded = folded + block[:, start : start + LANES]
    return line_sums(folded)


def line_sums(folded):
    lines = []
    for start in range(0, folded.shape[0], LANES):
        lines.append(jnp.sum(folded[start : start + LANES].T, 0, keepdims=True))
    return jnp.concatenate(lines, 0)


def exponentials(unit, direction):
    scores = lax.dot_general(
        unit, direction, (((1,), (1,)), ((), ())), preferred_element_type=jnp.float32
    )
    return jnp.exp(scores * (1.0 / student_temp) - 1.0 / student_temp)


def picked_kernel(nz, partner_ref, core_ref, own_ref, other_ref, mine_ref, theirs_ref, picked_ref, sums_ref, direction_ref, whole, folded, halves, sems):
    slab = pl.program_id(0)
    nx = pl.num_programs(0)
    half = own_ref.shape[0]
    ny, rows, protos = picked_ref.shape
    few = TILE // ny
    per_dp = rows // few // nz

    @pl.when(slab == 0)
    def _():
        owned = mine_ref.shape[0]
        moves = [
            pltpu.make_async_copy(own_ref, whole.at[pl.ds(0, half)], sems.at[0]),
            pltpu.make_async_copy(other_ref, whole.at[pl.ds(half, half)], sems.at[1]),
            pltpu.make_async_copy(mine_ref, halves.at[0], sems.at[2]),
            pltpu.make_async_copy(theirs_ref, halves.at[1], sems.at[3]),
        ]
        for move in moves:
            move.start()
        for move in moves:
            move.wait()
        leading = core_ref[0] == 0
        mine = halves[0].astype(jnp.float32)
        theirs = halves[1].astype(jnp.float32)
        direction_ref[:owned, :] = jnp.where(leading, mine, theirs).astype(jnp.bfloat16)
        direction_ref[owned:, :] = jnp.where(leading, theirs, mine).astype(jnp.bfloat16)

    shift = core_ref[0] * half
    for group in range(rows // TILE):
        loaded = []
        for k in range(group * ny, (group + 1) * ny):
            z, tile = divmod(k, per_dp)
            wanted = partner_ref[z * nx * per_dp + slab * per_dp + tile] + shift
            wanted = jnp.where(wanted >= 2 * half, wanted - 2 * half, wanted)
            loaded.append(whole[wanted].astype(jnp.float32))
        place = slice(group * TILE, (group + 1) * TILE)
        for y in range(ny):
            piece = jnp.concatenate([tile[y * few : (y + 1) * few] for tile in loaded], 0)
            picked_ref[y, place, :] = piece.astype(jnp.bfloat16)
            total = piece[:, :LANES]
            for start in range(LANES, protos, LANES):
                total = total + piece[:, start : start + LANES]
            folded[y * rows + group * TILE : y * rows + (group + 1) * TILE, :] = total
    sums_ref[0] = line_sums(folded[...])


def picked_sums(partner, core, own, other, mine, theirs, nz, nx, ny):
    half, _, protos = own.shape
    owned, embed = mine.shape
    rows = 2 * half * TILE // (nx * ny)
    lines = ny * rows // LANES
    return pl.pallas_call(
        functools.partial(picked_kernel, nz),
        grid_spec=pltpu.PrefetchScalarGridSpec(
            num_scalar_prefetch=2,
            grid=(nx,),
            in_specs=[pl.BlockSpec(memory_space=pltpu.HBM)] * 4,
            out_specs=[
                pl.BlockSpec((ny, rows, protos), lambda i, p, c: (i, 0, 0)),
                pl.BlockSpec((1, lines, LANES), lambda i, p, c: (i, 0, 0)),
                pl.BlockSpec((2 * owned, embed), lambda i, p, c: (0, 0)),
            ],
            scratch_shapes=[
                pltpu.VMEM((2 * half, TILE, protos), jnp.bfloat16),
                pltpu.VMEM((ny * rows, LANES), jnp.float32),
                pltpu.VMEM((2, owned, embed), jnp.bfloat16),
                pltpu.SemaphoreType.DMA((4,)),
            ],
        ),
        out_shape=[
            jax.ShapeDtypeStruct((nx * ny, rows, protos), jnp.bfloat16),
            jax.ShapeDtypeStruct((nx, lines, LANES), jnp.float32),
            jax.ShapeDtypeStruct((2 * owned, embed), jnp.bfloat16),
        ],
        compiler_params=pltpu.CompilerParams(vmem_limit_bytes=60 << 20),
    )(partner, core, own, other, mine, theirs)


def halves_stacked(rows):
    return jnp.concatenate([rows[:, :LANES], rows[:, LANES:]], 0)


def halves_joined(stack):
    rows = stack.shape[0] // 2
    return jnp.concatenate([stack[:rows], stack[rows:]], 1)


def small_call(kernel, shape, dtype, *operands, scalars=0):
    specs = [pl.BlockSpec(memory_space=pltpu.SMEM)] * scalars
    specs += [pl.BlockSpec(memory_space=pltpu.VMEM)] * (len(operands) - scalars)
    return pl.pallas_call(
        kernel,
        in_specs=specs,
        out_specs=pl.BlockSpec(memory_space=pltpu.VMEM),
        out_shape=jax.ShapeDtypeStruct(shape, dtype),
        compiler_params=pltpu.CompilerParams(vmem_limit_bytes=8 << 20),
    )(*operands)


def unit_kernel(ny, y_ref, features_ref, out_ref):
    feats = features_ref[0].astype(jnp.float32)
    length = jnp.sqrt(jnp.sum(feats * feats, 1, keepdims=True) + norm_eps)
    unit = feats / length
    few = TILE // ny
    chosen = None
    for y in range(ny):
        rows = [unit[t + y * few : t + (y + 1) * few] for t in range(0, feats.shape[0], TILE)]
        rows = jnp.concatenate(rows, 0)
        chosen = rows if chosen is None else jnp.where(y_ref[0] == y, rows, chosen)
    stack = halves_stacked(chosen).astype(jnp.bfloat16)
    for z in range(out_ref.shape[0]):
        out_ref[z] = stack


def outgoing_kernel(unit_ref, out_ref):
    pieces = [halves_joined(unit_ref[z].astype(jnp.float32)) for z in range(unit_ref.shape[0])]
    own = jnp.concatenate(pieces, 0).astype(jnp.bfloat16)
    for chunk in range(out_ref.shape[0]):
        out_ref[chunk] = own


def plane_sum_kernel(in_ref, out_ref):
    total = in_ref[0].astype(jnp.float32)
    for chunk in range(1, in_ref.shape[0]):
        total = total + in_ref[chunk].astype(jnp.float32)
    count = out_ref.shape[0]
    part = total.shape[0] // count
    for z in range(count):
        out_ref[z] = halves_stacked(total[z * part : (z + 1) * part])


def grad_kernel(dunit_ref, features_ref, out_ref):
    ny, stack, _ = dunit_ref.shape
    few = TILE // ny
    parts = [halves_joined(dunit_ref[y]) for y in range(ny)]
    rows = []
    for t in range(0, stack // 2, few):
        rows += [parts[y][t : t + few] for y in range(ny)]
    out_ref[0] = norm_back(jnp.concatenate(rows, 0), features_ref[0].astype(jnp.float32))


def expo_kernel(unit_ref, direction_ref, sums_ref, out_ref, found):
    step = pl.program_id(0)
    expo = exponentials(unit_ref[...], direction_ref[...])
    found[step] = row_sums(expo)

    @pl.when(step == pl.num_programs(0) - 1)
    def _():
        parts = [found[k] for k in range(found.shape[0])]
        parts += [sums_ref[k] for k in range(sums_ref.shape[0])]
        message = jnp.concatenate(parts, 0).astype(jnp.bfloat16)
        for z in range(out_ref.shape[0]):
            out_ref[z] = message


def expo_sums(unit_all, direction, target_sums, nz):
    crops, embed = unit_all.shape
    protos = direction.shape[0]
    lines = 2 * crops // LANES
    return pl.pallas_call(
        expo_kernel,
        grid=(crops // BLOCK,),
        in_specs=[
            pl.BlockSpec((BLOCK, embed), lambda i: (i, 0)),
            pl.BlockSpec((protos, embed), lambda i: (0, 0)),
            pl.BlockSpec(target_sums.shape, lambda i: (0, 0, 0)),
        ],
        out_specs=pl.BlockSpec((nz, lines, LANES), lambda i: (0, 0, 0)),
        out_shape=jax.ShapeDtypeStruct((nz, lines, LANES), jnp.bfloat16),
        scratch_shapes=[pltpu.VMEM((crops // BLOCK, BLOCK // LANES, LANES), jnp.float32)],
        compiler_params=pltpu.CompilerParams(vmem_limit_bytes=16 << 20),
    )(unit_all, direction, target_sums)


def sum_copies_kernel(in_ref, out_ref):
    total = in_ref[0].astype(jnp.float32)
    for z in range(1, in_ref.shape[0]):
        total = total + in_ref[z].astype(jnp.float32)
    for chunk in range(out_ref.shape[0]):
        out_ref[chunk] = total


def dscore_kernel(core_ref, totals_ref, unit_ref, direction_ref, picked_ref, dunit_ref, keep_ref, send_ref, scale, dscore, ddir):
    step = pl.program_id(0)
    steps, lines, _ = scale.shape

    @pl.when(step == 0)
    def _():
        total = totals_ref[0]
        for chunk in range(1, totals_ref.shape[0]):
            total = total + totals_ref[chunk]
        factor = total[steps * lines :] / total[: steps * lines]
        for k in range(steps):
            scale[k] = factor[k * lines : (k + 1) * lines]

    expo = exponentials(unit_ref[...], direction_ref[...])
    factors = scale[step]
    for line in range(lines):
        rows = slice(line * LANES, (line + 1) * LANES)
        column = jnp.broadcast_to(factors[line : line + 1], (LANES, LANES)).T
        for start in range(0, dscore.shape[1], LANES):
            cols = slice(start, start + LANES)
            gap = expo[rows, cols] * column - picked_ref[rows, cols].astype(jnp.float32)
            dscore[rows, cols] = (gap * (1.0 / student_temp)).astype(jnp.bfloat16)
    dunit = jnp.dot(dscore[...], direction_ref[...], preferred_element_type=jnp.float32)
    dunit_ref[...] = dunit.astype(jnp.bfloat16)
    product = lax.dot_general(
        dscore[...], unit_ref[...], (((0,), (0,)), ((), ())), preferred_element_type=jnp.float32
    )

    @pl.when(step == 0)
    def _():
        ddir[...] = product

    @pl.when(step > 0)
    def _():
        ddir[...] += product

    @pl.when(step == steps - 1)
    def _():
        owned = keep_ref.shape[0]
        leading = core_ref[0] == 0
        keep_ref[...] = jnp.where(leading, ddir[:owned, :], ddir[owned:, :])
        send_ref[...] = jnp.where(leading, ddir[owned:, :], ddir[:owned, :])


def dunit_ddir(core, totals, unit_all, direction, picked):
    crops, embed = unit_all.shape
    protos = direction.shape[0]
    return pl.pallas_call(
        dscore_kernel,
        grid=(crops // BLOCK,),
        in_specs=[
            pl.BlockSpec(memory_space=pltpu.SMEM),
            pl.BlockSpec(totals.shape, lambda i: (0, 0, 0)),
            pl.BlockSpec((BLOCK, embed), lambda i: (i, 0)),
            pl.BlockSpec((protos, embed), lambda i: (0, 0)),
            pl.BlockSpec((BLOCK, protos), lambda i: (i, 0)),
        ],
        out_specs=[
            pl.BlockSpec((BLOCK, embed), lambda i: (i, 0)),
            pl.BlockSpec((protos // 2, embed), lambda i: (0, 0)),
            pl.BlockSpec((protos // 2, embed), lambda i: (0, 0)),
        ],
        out_shape=[
            jax.ShapeDtypeStruct((crops, embed), jnp.bfloat16),
            jax.ShapeDtypeStruct((protos // 2, embed), jnp.float32),
            jax.ShapeDtypeStruct((protos // 2, embed), jnp.float32),
        ],
        scratch_shapes=[
            pltpu.VMEM((crops // BLOCK, BLOCK // LANES, LANES), jnp.float32),
            pltpu.VMEM((BLOCK, protos), jnp.bfloat16),
            pltpu.VMEM((protos, embed), jnp.float32),
        ],
        compiler_params=pltpu.CompilerParams(vmem_limit_bytes=16 << 20),
    )(core, totals, unit_all, direction, picked)


def per_device(features, targets, partner, vectors, first, second, teacher):
    nz, nx, ny = lax.axis_size("z"), lax.axis_size("x"), lax.axis_size("y")
    core = lax.axis_index("crop")[None].astype(jnp.int32)
    y_index = lax.axis_index("y")[None].astype(jnp.int32)
    own_rows, embed = features.shape[1:]
    part = own_rows // ny
    stack = 2 * part
    crops = nz * nx * own_rows
    chunks = nx * ny
    half, protos = targets.shape
    other = swapped(targets)
    unit_z = small_call(
        functools.partial(unit_kernel, ny),
        (nz, stack, LANES),
        jnp.bfloat16,
        y_index,
        features,
        scalars=1,
    )
    unit_z = exchanged(unit_z, "z")
    vlen = jnp.sqrt(jnp.sum(vectors * vectors, 1, keepdims=True) + norm_eps)
    own_direction = (vectors / vlen).astype(jnp.bfloat16)
    other_direction = swapped(own_direction)
    picked, target_sums, direction = picked_sums(
        partner[0],
        core,
        targets.reshape(half // TILE, TILE, protos),
        other.reshape(half // TILE, TILE, protos),
        own_direction,
        other_direction,
        nz,
        nx,
        ny,
    )
    unit_z, target_sums, picked, direction = lax.optimization_barrier(
        (unit_z, target_sums, picked, direction)
    )
    unit_all = small_call(outgoing_kernel, (chunks, nz * part, embed), jnp.bfloat16, unit_z)
    unit_all = exchanged(unit_all, PLANE).reshape(crops, embed)
    sums = exchanged(expo_sums(unit_all, direction, target_sums, nz), "z")
    totals = small_call(sum_copies_kernel, (chunks,) + sums.shape[1:], jnp.float32, sums)
    totals = exchanged(totals, PLANE)
    picked = picked.reshape(crops, protos)
    partial, ours, sent = dunit_ddir(core, totals, unit_all, direction, picked)
    theirs = swapped(sent)
    partial = exchanged(partial.reshape(chunks, nz * part, embed), PLANE)
    partial = small_call(plane_sum_kernel, (nz, stack, LANES), jnp.float32, partial)
    partial = exchanged(partial, "z")
    partial, theirs, ours = lax.optimization_barrier((partial, theirs, ours))
    partial = small_call(sum_copies_kernel, (ny, stack, LANES), jnp.float32, partial)
    dunit = exchanged(partial, "y")
    grad_rows = small_call(grad_kernel, features.shape, jnp.float32, dunit, features)
    new_vectors, new_first, new_second, new_teacher = adamw_rows(
        ours + theirs, vectors, first, second, teacher
    )
    return (grad_rows, new_vectors, new_first, new_second, new_teacher)


def solution(mesh):
    shape = mesh.devices.shape
    apart = Mesh(mesh.devices.reshape(shape[0] // 4, 4, shape[1], shape[2]), AXES)
    rows = P(("z", "x", "y", "crop"), None)
    crops = P("crop", ("z", "x"), None)
    return jax.shard_map(
        per_device,
        mesh=apart,
        in_specs=(
            crops,
            P("crop", ("z", "x", "y")),
            P("crop", None),
            rows,
            rows,
            rows,
            rows,
        ),
        out_specs=(crops, rows, rows, rows, rows),
        check_vma=False,
    )
```

profile of v0, /device:TPU:6, one launch (start us, length us, event | category | flops | bytes accessed | tf_op | source)
XLA Modules:
  0.0 160.2 jit_solution(11612364830225437349)
XLA Ops:
  0.6 1.9 %collective-permute-start = (bf16[1536,512]{1,0:T(8,128)(2,1)}, bf16[1536,512]{1,0:T(8,128)(2,1)S(1)}, u32[]{:S(2)}, u32[]{:S(2)}) collective-permute-start(bf16[1536,512]{1,0:T(8,128)(2,1)} %param.8), channel_id=1, source_target_pairs={{0,4},{4,0},{1,5},{5,1},{2,6},{6,2},{3,7},{7,3},{8,12},{12,8},{9,1... | collective-permute-start | bytes 4718600 | tf_op jit(solution)/shard_map/ppermute | solution.py:30
  3.3 0.7 shard_map.110
  4.1 15.2 %all-to-all-start = ((bf16[16,24,128]{2,1,0:T(8,128)(2,1)}), bf16[16,24,128]{2,1,0:T(8,128)(2,1)S(1)}, u32[]{:S(2)}, u32[]{:S(2)}) async-start(bf16[16,24,128]{2,1,0:T(8,128)(2,1)} %shard_map.110), calls=%async_computation | async-start | bytes 196608 | tf_op jit(solution)/shard_map/all_to_all | solution.py:34
  19.3 1.1 multiply_reduce_fusion.1
  20.3 1.1 fusion.1.mine_ref
  21.4 2.1 %collective-permute-start.1 = (bf16[256,256]{1,0:T(8,128)(2,1)S(1)}, bf16[256,256]{1,0:T(8,128)(2,1)S(1)}, u32[]{:S(2)}, u32[]{:S(2)}) collective-permute-start(bf16[256,256]{1,0:T(8,128)(2,1)S(1)} %fusion.1.mine_ref), channel_id=1, source_target_pairs={{0,4},{4,0},{1,5},{5,1},{2,6},{6,2},{3,7},{7,3},{8,12},{12,8},{9,1... | collective-permute-start | bytes 393224 | tf_op jit(solution)/shard_map/ppermute | solution.py:30
  23.6 1.1 collective-permute-done.1.theirs_ref
  25.9 5.4 %shard_map.111 = (bf16[16,192,512]{2,1,0:T(8,128)(2,1)}, f32[4,6,128]{2,1,0:T(8,128)}, bf16[512,256]{1,0:T(8,128)(2,1)}) custom-call(s32[192]{0:T(256)} %bitcast.14, s32[1]{0:T(128)} %bitcast.core_ref, bf16[96,16,512]{2,1,0:T(8,128)(2,1)} %bitcast.12, bf16[96,16,512]{2,1,0:T(8,128)(2,1)} %bitcast.13, bf16[256,256]{1,0:T(8,128)(2,1)} %copy-done.7, ...), custom_call_target="tpu_custom_call" | custom-call | tf_op jit(solution)/shard_map/pallas_call | solution.py:130
  31.2 1.6 %all-to-all-done.unit_ref = bf16[16,24,128]{2,1,0:T(8,128)(2,1)S(1)} async-done(((bf16[16,24,128]{2,1,0:T(8,128)(2,1)}), bf16[16,24,128]{2,1,0:T(8,128)(2,1)S(1)}, u32[]{:S(2)}, u32[]{:S(2)}) %all-to-all-start) | async-done | bytes 98336 | tf_op jit(solution)/shard_map/all_to_all | solution.py:34
  33.0 27.0 %all_to_all.35 = bf16[16,192,256]{2,1,0:T(8,128)(2,1)S(1)} all-to-all(bf16[16,192,256]{2,1,0:T(8,128)(2,1)S(1)} %shard_map.112), channel_id=1, replica_groups=mesh['z'=16,'x'=4,'crop'=2,'y'=4] {'x','y'}, dimensions={0} | all-to-all | bytes 3145728 | tf_op jit(solution)/shard_map/all_to_all | solution.py:34
  60.0 2.2 %shard_map.113 = bf16[16,48,128]{2,1,0:T(8,128)(2,1)S(1)} custom-call(bf16[3072,256]{1,0:T(8,128)(2,1)S(1)} %bitcast.8, bf16[512,256]{1,0:T(8,128)(2,1)S(1)} %copy-done.1, f32[4,6,128]{2,1,0:T(8,128)S(1)} %copy-done.4), custom_call_target="tpu_custom_call" | custom-call | tf_op jit(solution)/shard_map/pallas_call | solution.py:238
  62.2 27.1 %all_to_all.36.in_ref = bf16[16,48,128]{2,1,0:T(8,128)(2,1)S(1)} all-to-all(bf16[16,48,128]{2,1,0:T(8,128)(2,1)S(1)} %shard_map.113), channel_id=1, replica_groups=mesh['z'=16,'x'=4,'crop'=2,'y'=4] {'z'}, dimensions={0} | all-to-all | bytes 393216 | tf_op jit(solution)/shard_map/all_to_all | solution.py:34
  89.3 13.1 %all_to_all.37.totals_ref = f32[16,48,128]{2,1,0:T(8,128)S(1)} all-to-all(f32[16,48,128]{2,1,0:T(8,128)S(1)} %shard_map.114), channel_id=1, replica_groups=mesh['z'=16,'x'=4,'crop'=2,'y'=4] {'x','y'}, dimensions={0} | all-to-all | bytes 786432 | tf_op jit(solution)/shard_map/all_to_all | solution.py:34
  102.4 4.8 %shard_map.115 = (bf16[3072,256]{1,0:T(8,128)(2,1)S(1)}, f32[256,256]{1,0:T(8,128)S(1)}, f32[256,256]{1,0:T(8,128)S(1)}) custom-call(s32[1]{0:T(128)} %bitcast.core_ref, f32[16,48,128]{2,1,0:T(8,128)S(1)} %all_to_all.37.totals_ref, bf16[3072,256]{1,0:T(8,128)(2,1)S(1)} %bitcast.9, bf16[512,256]{1,0:T(8,128)(2,1)S(1)} %copy-done.1, bf16[3072,512]{1,0:T(8,128)(2,1)S(1)} %bitcast.10), custom_call_target="tpu_custom_call" | custom-call | tf_op jit(solution)/shard_map/pallas_call | solution.py:308
  107.3 19.9 %all_to_all.38.in_ref = bf16[16,192,256]{2,1,0:T(8,128)(2,1)S(1)} all-to-all(bf16[16,192,256]{2,1,0:T(8,128)(2,1)S(1)} %bitcast.11), channel_id=1, replica_groups=mesh['z'=16,'x'=4,'crop'=2,'y'=4] {'x','y'}, dimensions={0} | all-to-all | bytes 3145728 | tf_op jit(solution)/shard_map/all_to_all | solution.py:34
  127.1 0.9 shard_map.116
  128.0 8.4 %all-to-all-start.5 = ((f32[16,24,128]{2,1,0:T(8,128)}), f32[16,24,128]{2,1,0:T(8,128)S(1)}, u32[]{:S(2)}, u32[]{:S(2)}) async-start(f32[16,24,128]{2,1,0:T(8,128)} %shard_map.116), calls=%async_computation.5 | async-start | bytes 393216 | tf_op jit(solution)/shard_map/all_to_all | solution.py:34
  136.4 1.9 %collective-permute-start.2 = (f32[256,256]{1,0:T(8,128)S(1)}, f32[256,256]{1,0:T(8,128)S(1)}, u32[]{:S(2)}, u32[]{:S(2)}) collective-permute-start(f32[256,256]{1,0:T(8,128)S(1)} %get-tuple-element.26), channel_id=1, source_target_pairs={{0,4},{4,0},{1,5},{5,1},{2,6},{6,2},{3,7},{7,3},{8,12},{12,8},{9,1... | collective-permute-start | bytes 786440 | tf_op jit(solution)/shard_map/ppermute | solution.py:30
  138.3 1.5 collective-permute-done.2
  139.8 10.2 %all-to-all-done.5.in_ref = f32[16,24,128]{2,1,0:T(8,128)S(1)} async-done(((f32[16,24,128]{2,1,0:T(8,128)}), f32[16,24,128]{2,1,0:T(8,128)S(1)}, u32[]{:S(2)}, u32[]{:S(2)}) %all-to-all-start.5) | async-done | bytes 196640 | tf_op jit(solution)/shard_map/all_to_all | solution.py:34
  150.6 3.3 %all-to-all-start.6 = ((f32[4,24,128]{2,1,0:T(8,128)}), f32[4,24,128]{2,1,0:T(8,128)S(1)}, u32[]{:S(2)}, u32[]{:S(2)}) async-start(f32[4,24,128]{2,1,0:T(8,128)} %shard_map.117), calls=%async_computation.6 | async-start | bytes 98304 | tf_op jit(solution)/shard_map/all_to_all | solution.py:34
  154.2 1.3 multiply_add_fusion
  155.5 4.0 %all-to-all-done.6.dunit_ref = f32[4,24,128]{2,1,0:T(8,128)S(1)} async-done(((f32[4,24,128]{2,1,0:T(8,128)}), f32[4,24,128]{2,1,0:T(8,128)S(1)}, u32[]{:S(2)}, u32[]{:S(2)}) %all-to-all-start.6) | async-done | bytes 49184 | tf_op jit(solution)/shard_map/all_to_all | solution.py:34
  159.4 0.8 shard_map.118
  (30 shorter events, 3.0 us)
Async XLA Ops:
  0.6 24.0 %collective-permute-start = (bf16[1536,512]{1,0:T(8,128)(2,1)}, bf16[1536,512]{1,0:T(8,128)(2,1)S(1)}, u32[]{:S(2)}, u32[]{:S(2)}) collective-permute-start(bf16[1536,512]{1,0:T(8,128)(2,1)} %param.8), channel_id=1, source_target_pairs={{0,4},{4,0},{1,5},{5,1},{2,6},{6,2},{3,7},{7,3},{8,12},{12,8},{9,1... | collective-permute-start | bytes 4718600 | tf_op jit(solution)/shard_map/ppermute | solution.py:30
  2.6 0.7 copy-start.2
  4.1 28.8 %all-to-all-start = ((bf16[16,24,128]{2,1,0:T(8,128)(2,1)}), bf16[16,24,128]{2,1,0:T(8,128)(2,1)S(1)}, u32[]{:S(2)}, u32[]{:S(2)}) async-start(bf16[16,24,128]{2,1,0:T(8,128)(2,1)} %shard_map.110), calls=%async_computation | async-start | bytes 196608 | tf_op jit(solution)/shard_map/all_to_all | solution.py:34
  21.4 3.3 %copy-start.7 = (bf16[256,256]{1,0:T(8,128)(2,1)}, bf16[256,256]{1,0:T(8,128)(2,1)S(1)}, u32[]{:S(2)}) copy-start(bf16[256,256]{1,0:T(8,128)(2,1)S(1)} %fusion.1.mine_ref) | copy-start | bytes 393220
  21.4 3.2 %collective-permute-start.1 = (bf16[256,256]{1,0:T(8,128)(2,1)S(1)}, bf16[256,256]{1,0:T(8,128)(2,1)S(1)}, u32[]{:S(2)}, u32[]{:S(2)}) collective-permute-start(bf16[256,256]{1,0:T(8,128)(2,1)S(1)} %fusion.1.mine_ref), channel_id=1, source_target_pairs={{0,4},{4,0},{1,5},{5,1},{2,6},{6,2},{3,7},{7,3},{8,12},{12,8},{9,1... | collective-permute-start | bytes 393224 | tf_op jit(solution)/shard_map/ppermute | solution.py:30
  24.7 0.7 copy-start.11
  24.7 1.2 copy-start.6
  33.0 27.0 %copy-start.1 = (bf16[512,256]{1,0:T(8,128)(2,1)S(1)}, bf16[512,256]{1,0:T(8,128)(2,1)}, u32[]{:S(2)}) copy-start(bf16[512,256]{1,0:T(8,128)(2,1)} %get-tuple-element.22.direction_ref) | copy-start | bytes 786436
  33.0 27.0 %copy-start.4 = (f32[4,6,128]{2,1,0:T(8,128)S(1)}, f32[4,6,128]{2,1,0:T(8,128)}, u32[]{:S(2)}) copy-start(f32[4,6,128]{2,1,0:T(8,128)} %get-tuple-element.23.sums_ref) | copy-start | bytes 36868
  60.0 42.4 %copy-start = (bf16[16,192,512]{2,1,0:T(8,128)(2,1)S(1)}, bf16[16,192,512]{2,1,0:T(8,128)(2,1)}, u32[]{:S(2)}) copy-start(bf16[16,192,512]{2,1,0:T(8,128)(2,1)} %get-tuple-element.24) | copy-start | bytes 9437188
  127.1 26.8 %copy-start.5 = (f32[256,256]{1,0:T(8,128)S(1)}, f32[256,256]{1,0:T(8,128)}, u32[]{:S(2)}) copy-start(f32[256,256]{1,0:T(8,128)} %param.10) | copy-start | bytes 786436
  127.1 27.0 %copy-start.8 = (f32[256,256]{1,0:T(8,128)S(1)}, f32[256,256]{1,0:T(8,128)}, u32[]{:S(2)}) copy-start(f32[256,256]{1,0:T(8,128)} %param.13) | copy-start | bytes 786436
  127.1 27.0 %copy-start.9 = (f32[256,256]{1,0:T(8,128)S(1)}, f32[256,256]{1,0:T(8,128)}, u32[]{:S(2)}) copy-start(f32[256,256]{1,0:T(8,128)} %param.11) | copy-start | bytes 786436
  127.1 27.0 %copy-start.10 = (f32[256,256]{1,0:T(8,128)S(1)}, f32[256,256]{1,0:T(8,128)}, u32[]{:S(2)}) copy-start(f32[256,256]{1,0:T(8,128)} %param.12) | copy-start | bytes 786436
  128.0 22.0 %all-to-all-start.5 = ((f32[16,24,128]{2,1,0:T(8,128)}), f32[16,24,128]{2,1,0:T(8,128)S(1)}, u32[]{:S(2)}, u32[]{:S(2)}) async-start(f32[16,24,128]{2,1,0:T(8,128)} %shard_map.116), calls=%async_computation.5 | async-start | bytes 393216 | tf_op jit(solution)/shard_map/all_to_all | solution.py:34
  136.4 3.4 %collective-permute-start.2 = (f32[256,256]{1,0:T(8,128)S(1)}, f32[256,256]{1,0:T(8,128)S(1)}, u32[]{:S(2)}, u32[]{:S(2)}) collective-permute-start(f32[256,256]{1,0:T(8,128)S(1)} %get-tuple-element.26), channel_id=1, source_target_pairs={{0,4},{4,0},{1,5},{5,1},{2,6},{6,2},{3,7},{7,3},{8,12},{12,8},{9,1... | collective-permute-start | bytes 786440 | tf_op jit(solution)/shard_map/ppermute | solution.py:30
  150.6 8.8 %all-to-all-start.6 = ((f32[4,24,128]{2,1,0:T(8,128)}), f32[4,24,128]{2,1,0:T(8,128)S(1)}, u32[]{:S(2)}, u32[]{:S(2)}) async-start(f32[4,24,128]{2,1,0:T(8,128)} %shard_map.117), calls=%async_computation.6 | async-start | bytes 98304 | tf_op jit(solution)/shard_map/all_to_all | solution.py:34
  153.9 5.5 %copy-start.3 = (bf16[1,48,256]{2,1,0:T(8,128)(2,1)S(1)}, bf16[1,48,256]{2,1,0:T(8,128)(2,1)}, u32[]{:S(2)}) copy-start(bf16[1,48,256]{2,1,0:T(8,128)(2,1)} %features_ref.3) | copy-start | bytes 73732
where the time goes:
time: 162 us; the launch traced here: 160 us
  blocking collectives  87 us (54%)
  starting transfers between devices  32.8 us (20%)
  waiting for transfers between devices  18.3 us (11%)
  Pallas kernels  15.7 us (10%)
  other arithmetic  3.62 us (2%)
  local copies, waits for them, and re-layouts  1.97 us (1%)
    all_to_all x4, blocking collectives, exchanged(): return lax.all_to_all(blocks, axes, 0, 0, tiled=True)  87 us
    all_to_all x3, starting transfers between devices, exchanged(): return lax.all_to_all(blocks, axes, 0, 0, tiled=True)  26.8 us
    all_to_all x3, waiting for transfers between devices, exchanged(): return lax.all_to_all(blocks, axes, 0, 0, tiled=True)  15.7 us
    ppermute x3, starting transfers between devices, swapped(): return lax.ppermute(shard, 'crop', [(0, 1), (1, 0)])  5.97 us
    pallas_call x1, Pallas kernels, picked_sums(): pl.pallas_call(functools.partial(picked_kernel, nz), grid_spec=pltpu.Pref...  5.36 us
    pallas_call x1, Pallas kernels, dunit_ddir(): pl.pallas_call(dscore_kernel, grid=(crops // BLOCK,), in_specs=[pl.BlockS...  4.85 us
    pallas_call x6, Pallas kernels, small_call(): pl.pallas_call(kernel, in_specs=specs, out_specs=pl.BlockSpec(memory_spac...  3.27 us
  transfers between devices with their start and end apart: 6, of which 5 were waited for; matrix products, arithmetic and copies ran while one was open for 2% of the time, Pallas kernels for 4%

commit v1 on v0

v1 whole, which is shorter than its diff:
```python
import functools

import jax
import jax.numpy as jnp
from jax import lax
from jax.experimental import pallas as pl
from jax.experimental.pallas import tpu as pltpu
from jax.sharding import Mesh, PartitionSpec as P

TILE = 16
AXES = ("z", "x", "crop", "y")
PLANE = ("x", "y")
LANES = 128
BLOCK = 768


student_temp = 0.1
norm_eps = 1e-06
learn_rate = 0.01
weight_decay = 0.04
beta_first = 0.9
beta_second = 0.999
bias_first = 0.9999734386011124
bias_second = 0.0952078536
adam_eps = 1e-08
teacher_keep = 0.996


def swapped(shard):
    return lax.ppermute(shard, "crop", [(0, 1), (1, 0)])


def exchanged(blocks, axes):
    return lax.all_to_all(blocks, axes, 0, 0, tiled=True)


def norm_back(upstream, feats):
    length = jnp.sqrt(jnp.sum(feats * feats, 1, keepdims=True) + norm_eps)
    unit = feats / length
    return (upstream - unit * jnp.sum(unit * upstream, 1, keepdims=True)) / length


def adamw_rows(grad_rows, vectors, first, second, teacher):
    vlen = jnp.sqrt(jnp.sum(vectors * vectors, 1, keepdims=True) + norm_eps)
    unit = vectors / vlen
    dvec = (grad_rows - unit * jnp.sum(unit * grad_rows, 1, keepdims=True)) / vlen
    new_first = beta_first * first + (1.0 - beta_first) * dvec
    new_second = beta_second * second + (1.0 - beta_second) * dvec * dvec
    update = (
        new_first / bias_first / (jnp.sqrt(new_second / bias_second) + adam_eps)
        + weight_decay * vectors
    )
    new_vectors = vectors - learn_rate * update
    new_teacher = teacher_keep * teacher + (1.0 - teacher_keep) * new_vectors
    return (new_vectors, new_first, new_second, new_teacher)


def row_sums(block):
    folded = block[:, :LANES]
    for start in range(LANES, block.shape[1], LANES):
        folded = folded + block[:, start : start + LANES]
    return line_sums(folded)


def line_sums(folded):
    lines = []
    for start in range(0, folded.shape[0], LANES):
        lines.append(jnp.sum(folded[start : start + LANES].T, 0, keepdims=True))
    return jnp.concatenate(lines, 0)


def exponentials(unit, direction):
    scores = lax.dot_general(
        unit, direction, (((1,), (1,)), ((), ())), preferred_element_type=jnp.float32
    )
    return jnp.exp(scores * (1.0 / student_temp) - 1.0 / student_temp)


def picked_kernel(nz, partner_ref, core_ref, own_ref, other_ref, picked_ref, sums_ref, whole, folded, sems):
    slab = pl.program_id(0)
    nx = pl.num_programs(0)
    half = own_ref.shape[0]
    ny, rows, protos = picked_ref.shape
    few = TILE // ny
    per_dp = rows // few // nz

    @pl.when(slab == 0)
    def _():
        moves = [
            pltpu.make_async_copy(own_ref, whole.at[pl.ds(0, half)], sems.at[0]),
            pltpu.make_async_copy(other_ref, whole.at[pl.ds(half, half)], sems.at[1]),
        ]
        for move in moves:
            move.start()
        for move in moves:
            move.wait()

    shift = core_ref[0] * half
    for group in range(rows // TILE):
        loaded = []
        for k in range(group * ny, (group + 1) * ny):
            z, tile = divmod(k, per_dp)
            wanted = partner_ref[z * nx * per_dp + slab * per_dp + tile] + shift
            wanted = jnp.where(wanted >= 2 * half, wanted - 2 * half, wanted)
            loaded.append(whole[wanted].astype(jnp.float32))
        place = slice(group * TILE, (group + 1) * TILE)
        for y in range(ny):
            piece = jnp.concatenate([tile[y * few : (y + 1) * few] for tile in loaded], 0)
            picked_ref[y, place, :] = piece.astype(jnp.bfloat16)
            total = piece[:, :LANES]
            for start in range(LANES, protos, LANES):
                total = total + piece[:, start : start + LANES]
            folded[y * rows + group * TILE : y * rows + (group + 1) * TILE, :] = total
    sums_ref[0] = line_sums(folded[...])


def picked_sums(partner, core, own, other, nz, nx, ny):
    half, _, protos = own.shape
    rows = 2 * half * TILE // (nx * ny)
    lines = ny * rows // LANES
    return pl.pallas_call(
        functools.partial(picked_kernel, nz),
        grid_spec=pltpu.PrefetchScalarGridSpec(
            num_scalar_prefetch=2,
            grid=(nx,),
            in_specs=[pl.BlockSpec(memory_space=pltpu.HBM)] * 2,
            out_specs=[
                pl.BlockSpec((ny, rows, protos), lambda i, p, c: (i, 0, 0)),
                pl.BlockSpec((1, lines, LANES), lambda i, p, c: (i, 0, 0)),
            ],
            scratch_shapes=[
                pltpu.VMEM((2 * half, TILE, protos), jnp.bfloat16),
                pltpu.VMEM((ny * rows, LANES), jnp.float32),
                pltpu.SemaphoreType.DMA((2,)),
            ],
        ),
        out_shape=[
            jax.ShapeDtypeStruct((nx * ny, rows, protos), jnp.bfloat16),
            jax.ShapeDtypeStruct((nx, lines, LANES), jnp.float32),
        ],
        compiler_params=pltpu.CompilerParams(vmem_limit_bytes=60 << 20),
    )(partner, core, own, other)


def halves_stacked(rows):
    return jnp.concatenate([rows[:, :LANES], rows[:, LANES:]], 0)


def halves_joined(stack):
    rows = stack.shape[0] // 2
    return jnp.concatenate([stack[:rows], stack[rows:]], 1)


def plain_call(kernel, outs, *operands, scalars=0, scratch=(), limit=8):
    specs = [pl.BlockSpec(memory_space=pltpu.SMEM)] * scalars
    specs += [pl.BlockSpec(memory_space=pltpu.VMEM)] * (len(operands) - scalars)
    return pl.pallas_call(
        kernel,
        in_specs=specs,
        out_specs=[pl.BlockSpec(memory_space=pltpu.VMEM)] * len(outs),
        out_shape=[jax.ShapeDtypeStruct(*out) for out in outs],
        scratch_shapes=list(scratch),
        compiler_params=pltpu.CompilerParams(vmem_limit_bytes=limit << 20),
    )(*operands)


def small_call(kernel, shape, dtype, *operands, scalars=0):
    return plain_call(kernel, [(shape, dtype)], *operands, scalars=scalars)[0]


def direction_kernel(vectors_ref, out_ref):
    vectors = vectors_ref[...]
    vlen = jnp.sqrt(jnp.sum(vectors * vectors, 1, keepdims=True) + norm_eps)
    out_ref[...] = (vectors / vlen).astype(jnp.bfloat16)


def unit_kernel(ny, y_ref, features_ref, out_ref):
    feats = features_ref[0].astype(jnp.float32)
    length = jnp.sqrt(jnp.sum(feats * feats, 1, keepdims=True) + norm_eps)
    unit = feats / length
    few = TILE // ny
    chosen = None
    for y in range(ny):
        rows = [unit[t + y * few : t + (y + 1) * few] for t in range(0, feats.shape[0], TILE)]
        rows = jnp.concatenate(rows, 0)
        chosen = rows if chosen is None else jnp.where(y_ref[0] == y, rows, chosen)
    stack = halves_stacked(chosen).astype(jnp.bfloat16)
    for z in range(out_ref.shape[0]):
        out_ref[z] = stack


def outgoing_kernel(unit_ref, out_ref):
    pieces = [halves_joined(unit_ref[z].astype(jnp.float32)) for z in range(unit_ref.shape[0])]
    own = jnp.concatenate(pieces, 0).astype(jnp.bfloat16)
    for chunk in range(out_ref.shape[0]):
        out_ref[chunk] = own


def plane_sum_kernel(in_ref, out_ref):
    total = in_ref[0].astype(jnp.float32)
    for chunk in range(1, in_ref.shape[0]):
        total = total + in_ref[chunk].astype(jnp.float32)
    count = out_ref.shape[0]
    part = total.shape[0] // count
    for z in range(count):
        out_ref[z] = halves_stacked(total[z * part : (z + 1) * part])


def grad_kernel(dunit_ref, features_ref, out_ref):
    ny, stack, _ = dunit_ref.shape
    few = TILE // ny
    parts = [halves_joined(dunit_ref[y]) for y in range(ny)]
    rows = []
    for t in range(0, stack // 2, few):
        rows += [parts[y][t : t + few] for y in range(ny)]
    out_ref[0] = norm_back(jnp.concatenate(rows, 0), features_ref[0].astype(jnp.float32))


def expo_kernel(core_ref, unit_ref, mine_ref, theirs_ref, sums_ref, out_ref, direction_ref, expo_ref, found):
    owned = mine_ref.shape[0]
    leading = core_ref[0] == 0
    mine = mine_ref[...].astype(jnp.float32)
    theirs = theirs_ref[...].astype(jnp.float32)
    direction_ref[:owned, :] = jnp.where(leading, mine, theirs).astype(jnp.bfloat16)
    direction_ref[owned:, :] = jnp.where(leading, theirs, mine).astype(jnp.bfloat16)

    def block(step, carry):
        rows = pl.ds(pl.multiple_of(step * BLOCK, BLOCK), BLOCK)
        expo = exponentials(unit_ref[rows, :], direction_ref[...])
        expo_ref[rows, :] = expo
        found[step] = row_sums(expo)
        return carry

    lax.fori_loop(0, found.shape[0], block, 0)
    parts = [found[k] for k in range(found.shape[0])]
    parts += [sums_ref[k] for k in range(sums_ref.shape[0])]
    message = jnp.concatenate(parts, 0).astype(jnp.bfloat16)
    for z in range(out_ref.shape[0]):
        out_ref[z] = message


def expo_sums(core, unit_all, mine, theirs, target_sums, nz):
    crops, embed = unit_all.shape
    return plain_call(
        expo_kernel,
        [
            ((nz, 2 * crops // LANES, LANES), jnp.bfloat16),
            ((2 * mine.shape[0], embed), jnp.bfloat16),
            ((crops, 2 * mine.shape[0]), jnp.float32),
        ],
        core,
        unit_all,
        mine,
        theirs,
        target_sums,
        scalars=1,
        scratch=[pltpu.VMEM((crops // BLOCK, BLOCK // LANES, LANES), jnp.float32)],
        limit=16,
    )


def sum_copies_kernel(in_ref, out_ref):
    total = in_ref[0].astype(jnp.float32)
    for z in range(1, in_ref.shape[0]):
        total = total + in_ref[z].astype(jnp.float32)
    for chunk in range(out_ref.shape[0]):
        out_ref[chunk] = total.astype(out_ref.dtype)


def dscore_kernel(totals_ref, expo_ref, direction_ref, picked_ref, dunit_ref, dscore_ref, scale):
    steps, lines, _ = scale.shape
    total = totals_ref[0].astype(jnp.float32)
    for chunk in range(1, totals_ref.shape[0]):
        total = total + totals_ref[chunk].astype(jnp.float32)
    factor = total[steps * lines :] / total[: steps * lines]
    for k in range(steps):
        scale[k] = factor[k * lines : (k + 1) * lines]

    def block(step, carry):
        first = pl.multiple_of(step * BLOCK, BLOCK)
        own = pl.ds(first, BLOCK)
        factors = scale[step]
        for line in range(lines):
            rows = pl.ds(pl.multiple_of(first + line * LANES, LANES), LANES)
            column = jnp.broadcast_to(factors[line : line + 1], (LANES, LANES)).T
            for start in range(0, dscore_ref.shape[1], LANES):
                cols = slice(start, start + LANES)
                gap = expo_ref[rows, cols] * column - picked_ref[rows, cols].astype(jnp.float32)
                dscore_ref[rows, cols] = (gap * (1.0 / student_temp)).astype(jnp.bfloat16)
        dunit = jnp.dot(dscore_ref[own, :], direction_ref[...], preferred_element_type=jnp.float32)
        dunit_ref[own, :] = dunit.astype(jnp.bfloat16)
        return carry

    lax.fori_loop(0, steps, block, 0)


def dscore_dunit(totals, expo, direction, picked):
    crops, protos = expo.shape
    return plain_call(
        dscore_kernel,
        [((crops, direction.shape[1]), jnp.bfloat16), ((crops, protos), jnp.bfloat16)],
        totals,
        expo,
        direction,
        picked,
        scratch=[pltpu.VMEM((crops // BLOCK, BLOCK // LANES, LANES), jnp.float32)],
        limit=24,
    )


def ddir_kernel(core_ref, dscore_ref, unit_ref, keep_ref, send_ref):
    ddir = jnp.zeros((dscore_ref.shape[1], unit_ref.shape[1]), jnp.float32)
    for first in range(0, dscore_ref.shape[0], BLOCK):
        ddir = ddir + lax.dot_general(
            dscore_ref[first : first + BLOCK, :],
            unit_ref[first : first + BLOCK, :],
            (((0,), (0,)), ((), ())),
            preferred_element_type=jnp.float32,
        )
    owned = keep_ref.shape[0]
    leading = core_ref[0] == 0
    keep_ref[...] = jnp.where(leading, ddir[:owned], ddir[owned:])
    send_ref[...] = jnp.where(leading, ddir[owned:], ddir[:owned])


def per_device(features, targets, partner, vectors, first, second, teacher):
    nz, nx, ny = lax.axis_size("z"), lax.axis_size("x"), lax.axis_size("y")
    core = lax.axis_index("crop")[None].astype(jnp.int32)
    y_index = lax.axis_index("y")[None].astype(jnp.int32)
    own_rows, embed = features.shape[1:]
    part = own_rows // ny
    stack = 2 * part
    crops = nz * nx * own_rows
    chunks = nx * ny
    half, protos = targets.shape
    other = swapped(targets)
    unit_z = small_call(
        functools.partial(unit_kernel, ny),
        (nz, stack, LANES),
        jnp.bfloat16,
        y_index,
        features,
        scalars=1,
    )
    unit_z = exchanged(unit_z, "z")
    unit_z, vectors, own_targets = lax.optimization_barrier((unit_z, vectors, targets))
    own_direction = small_call(direction_kernel, vectors.shape, jnp.bfloat16, vectors)
    other_direction = swapped(own_direction)
    picked, target_sums = picked_sums(
        partner[0],
        core,
        own_targets.reshape(half // TILE, TILE, protos),
        other.reshape(half // TILE, TILE, protos),
        nz,
        nx,
        ny,
    )
    unit_all = small_call(outgoing_kernel, (chunks, nz * part, embed), jnp.bfloat16, unit_z)
    unit_all = exchanged(unit_all, PLANE).reshape(crops, embed)
    sums, direction, expo = expo_sums(core, unit_all, own_direction, other_direction, target_sums, nz)
    sums = exchanged(sums, "z")
    totals = small_call(sum_copies_kernel, (chunks,) + sums.shape[1:], jnp.bfloat16, sums)
    totals = exchanged(totals, PLANE)
    picked = picked.reshape(crops, protos)
    partial, dscore = dscore_dunit(totals, expo, direction, picked)
    partial = exchanged(partial.reshape(chunks, nz * part, embed), PLANE)
    partial, dscore = lax.optimization_barrier((partial, dscore))
    half_rows = (vectors.shape, jnp.float32)
    ours, sent = plain_call(
        ddir_kernel, [half_rows, half_rows], core, dscore, unit_all, scalars=1, limit=16
    )
    theirs = swapped(sent)
    partial = small_call(plane_sum_kernel, (nz, stack, LANES), jnp.float32, partial)
    partial = exchanged(partial, "z")
    partial, theirs, ours = lax.optimization_barrier((partial, theirs, ours))
    partial = small_call(sum_copies_kernel, (ny, stack, LANES), jnp.float32, partial)
    dunit = exchanged(partial, "y")
    grad_rows = small_call(grad_kernel, features.shape, jnp.float32, dunit, features)
    new_vectors, new_first, new_second, new_teacher = adamw_rows(
        ours + theirs, vectors, first, second, teacher
    )
    return (grad_rows, new_vectors, new_first, new_second, new_teacher)


def solution(mesh):
    shape = mesh.devices.shape
    apart = Mesh(mesh.devices.reshape(shape[0] // 4, 4, shape[1], shape[2]), AXES)
    rows = P(("z", "x", "y", "crop"), None)
    crops = P("crop", ("z", "x"), None)
    return jax.shard_map(
        per_device,
        mesh=apart,
        in_specs=(
            crops,
            P("crop", ("z", "x", "y")),
            P("crop", None),
            rows,
            rows,
            rows,
            rows,
        ),
        out_specs=(crops, rows, rows, rows, rows),
        check_vma=False,
    )
```

time: 162 us -> 153 us (0.944)
  blocking collectives: 87 us -> 51.5 us
  waiting for transfers between devices: 18.3 us -> 35.9 us
  starting transfers between devices: 32.8 us -> 40 us
  local copies, waits for them, and re-layouts: 1.97 us -> 5.26 us
  other arithmetic: 3.62 us -> 1.62 us
    all_to_all x4 -> x3, blocking collectives: 87 us -> 51.5 us  [exchanged(): return lax.all_to_all(blocks, axes, 0, 0, tiled=True)]
    all_to_all x3 -> x4, waiting for transfers between devices: 15.7 us -> 34.5 us  [exchanged(): return lax.all_to_all(blocks, axes, 0, 0, tiled=True)]
    all_to_all x3 -> x4, starting transfers between devices: 26.8 us -> 34.1 us  [exchanged(): return lax.all_to_all(blocks, axes, 0, 0, tiled=True)]
    unnamed x24 -> x20, local copies, waits for them, and re-layouts: 1.97 us -> 5.26 us
    pallas_call x8 -> x10, Pallas kernels: 10.3 us -> 10.7 us  [plain_call(): pl.pallas_call(kernel, in_specs=specs, out_specs=[pl.BlockSpec(memory_spa...]
  transfers between devices with their start and end apart: 6 -> 7, of which waited for: 5 -> 5; matrix products, arithmetic and copies ran while one was open for 2% -> 1% of each run, Pallas kernels for 4% -> 5%
where the time goes in v1:
time: 153 us; the launch traced here: 151 us
  blocking collectives  51.5 us (34%)
  starting transfers between devices  40 us (26%)
  waiting for transfers between devices  35.9 us (23%)
  Pallas kernels  15.9 us (10%)
  local copies, waits for them, and re-layouts  5.26 us (3%)
  other arithmetic  1.62 us (1%)
    all_to_all x3, blocking collectives, exchanged(): return lax.all_to_all(blocks, axes, 0, 0, tiled=True)  51.5 us
    all_to_all x4, waiting for transfers between devices, exchanged(): return lax.all_to_all(blocks, axes, 0, 0, tiled=True)  34.5 us
    all_to_all x4, starting transfers between devices, exchanged(): return lax.all_to_all(blocks, axes, 0, 0, tiled=True)  34.1 us
    pallas_call x10, Pallas kernels, plain_call(): pl.pallas_call(kernel, in_specs=specs, out_specs=[pl.BlockSpec(memory_spa...  10.7 us
    ppermute x3, starting transfers between devices, swapped(): return lax.ppermute(shard, 'crop', [(0, 1), (1, 0)])  5.9 us
    unnamed x20, local copies, waits for them, and re-layouts  5.26 us
    pallas_call x1, Pallas kernels, picked_sums(): pl.pallas_call(functools.partial(picked_kernel, nz), grid_spec=pltpu.Pref...  5.21 us
  transfers between devices with their start and end apart: 7, of which 5 were waited for; matrix products, arithmetic and copies ran while one was open for 1% of the time, Pallas kernels for 5%

profile of v1, /device:TPU:6, one launch (start us, length us, event | category | flops | bytes accessed | tf_op | source)
XLA Modules:
  0.0 151.0 jit_solution(12240349392376847611)
XLA Ops:
  2.1 15.2 %all-to-all-start = ((bf16[16,24,128]{2,1,0:T(8,128)(2,1)}), bf16[16,24,128]{2,1,0:T(8,128)(2,1)S(1)}, u32[]{:S(2)}, u32[]{:S(2)}) async-start(bf16[16,24,128]{2,1,0:T(8,128)(2,1)} %shard_map.110), calls=%async_computation | async-start | bytes 196608 | tf_op jit(solution)/shard_map/all_to_all | solution.py:34
  17.3 1.9 %collective-permute-start.1 = (bf16[1536,512]{1,0:T(8,128)(2,1)}, bf16[1536,512]{1,0:T(8,128)(2,1)}, u32[]{:S(2)}, u32[]{:S(2)}) collective-permute-start(bf16[1536,512]{1,0:T(8,128)(2,1)} %param.8), channel_id=1, source_target_pairs={{0,4},{4,0},{1,5},{5,1},{2,6},{6,2},{3,7},{7,3},{8,12},{12,8},{9,1... | collective-permute-start | bytes 4718600 | tf_op jit(solution)/shard_map/ppermute | solution.py:30
  19.3 11.6 %all-to-all-done.unit_ref = bf16[16,24,128]{2,1,0:T(8,128)(2,1)S(1)} async-done(((bf16[16,24,128]{2,1,0:T(8,128)(2,1)}), bf16[16,24,128]{2,1,0:T(8,128)(2,1)S(1)}, u32[]{:S(2)}, u32[]{:S(2)}) %all-to-all-start) | async-done | bytes 98336 | tf_op jit(solution)/shard_map/all_to_all | solution.py:34
  30.9 1.3 shard_map.111
  32.2 7.6 %all-to-all-start.1 = ((bf16[16,192,256]{2,1,0:T(8,128)(2,1)}), bf16[16,192,256]{2,1,0:T(8,128)(2,1)S(1)}, u32[]{:S(2)}, u32[]{:S(2)}) async-start(bf16[16,192,256]{2,1,0:T(8,128)(2,1)} %shard_map.111), calls=%async_computation.1 | async-start | bytes 3145728 | tf_op jit(solution)/shard_map/all_to_all | solution.py:34
  39.9 1.9 %collective-permute-start = (bf16[256,256]{1,0:T(8,128)(2,1)S(1)}, bf16[256,256]{1,0:T(8,128)(2,1)S(1)}, u32[]{:S(2)}, u32[]{:S(2)}) collective-permute-start(bf16[256,256]{1,0:T(8,128)(2,1)S(1)} %shard_map.112.mine_ref), channel_id=1, source_target_pairs={{0,4},{4,0},{1,5},{5,1},{2,6},{6,2},{3,7},{7,3},{8,12},{12,8},{9,1... | collective-permute-start | bytes 393224 | tf_op jit(solution)/shard_map/ppermute | solution.py:30
  41.9 5.2 %shard_map.113 = (bf16[16,192,512]{2,1,0:T(8,128)(2,1)}, f32[4,6,128]{2,1,0:T(8,128)}) custom-call(s32[192]{0:T(256)} %bitcast.13, s32[1]{0:T(128)} %bitcast.core_ref, bf16[96,16,512]{2,1,0:T(8,128)(2,1)} %bitcast.12, bf16[96,16,512]{2,1,0:T(8,128)(2,1)} %bitcast.5.other_ref), custom_call_target="tpu_custom_call" | custom-call | tf_op jit(solution)/shard_map/pallas_call | solution.py:121
  47.1 11.9 %all-to-all-done.1 = bf16[16,192,256]{2,1,0:T(8,128)(2,1)S(1)} async-done(((bf16[16,192,256]{2,1,0:T(8,128)(2,1)}), bf16[16,192,256]{2,1,0:T(8,128)(2,1)S(1)}, u32[]{:S(2)}, u32[]{:S(2)}) %all-to-all-start.1) | async-done | bytes 1572896 | tf_op jit(solution)/shard_map/all_to_all | solution.py:34
  59.7 2.2 %shard_map.114 = (bf16[16,48,128]{2,1,0:T(8,128)(2,1)S(1)}, bf16[512,256]{1,0:T(8,128)(2,1)S(1)}, f32[3072,512]{1,0:T(8,128)S(1)}) custom-call(s32[1]{0:T(128)} %bitcast.core_ref, bf16[3072,256]{1,0:T(8,128)(2,1)S(1)} %bitcast.8, bf16[256,256]{1,0:T(8,128)(2,1)S(1)} %shard_map.112.mine_ref, bf16[256,256]{1,0:T(8,128)(2,1)S(1)} %collective-permute-done.theirs_ref, ...), custom_call_target="tpu_custom_call" | custom-call | tf_op jit(solution)/shard_map/pallas_call | solution.py:157
  61.9 20.3 %all_to_all.35.in_ref = bf16[16,48,128]{2,1,0:T(8,128)(2,1)S(1)} all-to-all(bf16[16,48,128]{2,1,0:T(8,128)(2,1)S(1)} %get-tuple-element.26), channel_id=1, replica_groups=mesh['z'=16,'x'=4,'crop'=2,'y'=4] {'z'}, dimensions={0} | all-to-all | bytes 393216 | tf_op jit(solution)/shard_map/all_to_all | solution.py:34
  82.3 12.0 %all_to_all.36.totals_ref = bf16[16,48,128]{2,1,0:T(8,128)(2,1)S(1)} all-to-all(bf16[16,48,128]{2,1,0:T(8,128)(2,1)S(1)} %shard_map.115), channel_id=1, replica_groups=mesh['z'=16,'x'=4,'crop'=2,'y'=4] {'x','y'}, dimensions={0} | all-to-all | bytes 393216 | tf_op jit(solution)/shard_map/all_to_all | solution.py:34
  94.3 1.9 %copy-done.3 = bf16[16,192,512]{2,1,0:T(8,128)(2,1)S(1)} copy-done((bf16[16,192,512]{2,1,0:T(8,128)(2,1)S(1)}, bf16[16,192,512]{2,1,0:T(8,128)(2,1)}, u32[]{:S(2)}) %copy-start.3) | copy-done | bytes 3145752
  96.2 2.8 %shard_map.116 = (bf16[3072,256]{1,0:T(8,128)(2,1)S(1)}, bf16[3072,512]{1,0:T(8,128)(2,1)S(1)}) custom-call(bf16[16,48,128]{2,1,0:T(8,128)(2,1)S(1)} %all_to_all.36.totals_ref, f32[3072,512]{1,0:T(8,128)S(1)} %get-tuple-element.27.expo_ref, bf16[512,256]{1,0:T(8,128)(2,1)S(1)} %get-tuple-element.28.direction_ref, bf16[3072,512]{1,0:T(8,128)(2,1)S(1)} %bitcast.10), custom_call_target="tpu_custom_call" | custom-call | tf_op jit(solution)/shard_map/pallas_call | solution.py:157
  99.0 19.2 %all_to_all.37.in_ref = bf16[16,192,256]{2,1,0:T(8,128)(2,1)S(1)} all-to-all(bf16[16,192,256]{2,1,0:T(8,128)(2,1)S(1)} %bitcast.11), channel_id=1, replica_groups=mesh['z'=16,'x'=4,'crop'=2,'y'=4] {'x','y'}, dimensions={0} | all-to-all | bytes 3145728 | tf_op jit(solution)/shard_map/all_to_all | solution.py:34
  118.2 0.9 shard_map.117
  119.1 8.1 %all-to-all-start.5 = ((f32[16,24,128]{2,1,0:T(8,128)}), f32[16,24,128]{2,1,0:T(8,128)S(1)}, u32[]{:S(2)}, u32[]{:S(2)}) async-start(f32[16,24,128]{2,1,0:T(8,128)} %shard_map.117), calls=%async_computation.5 | async-start | bytes 393216 | tf_op jit(solution)/shard_map/all_to_all | solution.py:34
  127.2 1.9 %copy-done.2 = bf16[3072,512]{1,0:T(8,128)(2,1)S(1)} copy-done((bf16[3072,512]{1,0:T(8,128)(2,1)S(1)}, bf16[3072,512]{1,0:T(8,128)(2,1)}, u32[]{:S(2)}) %copy-start.2) | copy-done | bytes 3145752
  129.1 1.0 shard_map.118
  130.2 2.1 %collective-permute-start.2 = (f32[256,256]{1,0:T(8,128)S(1)}, f32[256,256]{1,0:T(8,128)S(1)}, u32[]{:S(2)}, u32[]{:S(2)}) collective-permute-start(f32[256,256]{1,0:T(8,128)S(1)} %get-tuple-element.34), channel_id=1, source_target_pairs={{0,4},{4,0},{1,5},{5,1},{2,6},{6,2},{3,7},{7,3},{8,12},{12,8},{9,1... | collective-permute-start | bytes 786440 | tf_op jit(solution)/shard_map/ppermute | solution.py:30
  132.3 1.4 collective-permute-done.2
  133.7 7.0 %all-to-all-done.5.in_ref = f32[16,24,128]{2,1,0:T(8,128)S(1)} async-done(((f32[16,24,128]{2,1,0:T(8,128)}), f32[16,24,128]{2,1,0:T(8,128)S(1)}, u32[]{:S(2)}, u32[]{:S(2)}) %all-to-all-start.5) | async-done | bytes 196640 | tf_op jit(solution)/shard_map/all_to_all | solution.py:34
  141.4 3.3 %all-to-all-start.6 = ((f32[4,24,128]{2,1,0:T(8,128)}), f32[4,24,128]{2,1,0:T(8,128)S(1)}, u32[]{:S(2)}, u32[]{:S(2)}) async-start(f32[4,24,128]{2,1,0:T(8,128)} %shard_map.119), calls=%async_computation.6 | async-start | bytes 98304 | tf_op jit(solution)/shard_map/all_to_all | solution.py:34
  144.9 1.3 multiply_add_fusion
  146.2 4.0 %all-to-all-done.6.dunit_ref = f32[4,24,128]{2,1,0:T(8,128)S(1)} async-done(((f32[4,24,128]{2,1,0:T(8,128)}), f32[4,24,128]{2,1,0:T(8,128)S(1)}, u32[]{:S(2)}, u32[]{:S(2)}) %all-to-all-start.6) | async-done | bytes 49184 | tf_op jit(solution)/shard_map/all_to_all | solution.py:34
  (28 shorter events, 4.2 us)
Async XLA Ops:
  0.6 0.7 copy-start.4
  2.1 28.8 %all-to-all-start = ((bf16[16,24,128]{2,1,0:T(8,128)(2,1)}), bf16[16,24,128]{2,1,0:T(8,128)(2,1)S(1)}, u32[]{:S(2)}, u32[]{:S(2)}) async-start(bf16[16,24,128]{2,1,0:T(8,128)(2,1)} %shard_map.110), calls=%async_computation | async-start | bytes 196608 | tf_op jit(solution)/shard_map/all_to_all | solution.py:34
  17.3 24.5 %collective-permute-start.1 = (bf16[1536,512]{1,0:T(8,128)(2,1)}, bf16[1536,512]{1,0:T(8,128)(2,1)}, u32[]{:S(2)}, u32[]{:S(2)}) collective-permute-start(bf16[1536,512]{1,0:T(8,128)(2,1)} %param.8), channel_id=1, source_target_pairs={{0,4},{4,0},{1,5},{5,1},{2,6},{6,2},{3,7},{7,3},{8,12},{12,8},{9,1... | collective-permute-start | bytes 4718600 | tf_op jit(solution)/shard_map/ppermute | solution.py:30
  32.2 7.6 %copy-start = (f32[256,256]{1,0:T(8,128)S(1)}, f32[256,256]{1,0:T(8,128)}, u32[]{:S(2)}) copy-start(f32[256,256]{1,0:T(8,128)} %vectors_ref) | copy-start | bytes 786436
  32.2 26.8 %all-to-all-start.1 = ((bf16[16,192,256]{2,1,0:T(8,128)(2,1)}), bf16[16,192,256]{2,1,0:T(8,128)(2,1)S(1)}, u32[]{:S(2)}, u32[]{:S(2)}) async-start(bf16[16,192,256]{2,1,0:T(8,128)(2,1)} %shard_map.111), calls=%async_computation.1 | async-start | bytes 3145728 | tf_op jit(solution)/shard_map/all_to_all | solution.py:34
  39.9 7.2 %collective-permute-start = (bf16[256,256]{1,0:T(8,128)(2,1)S(1)}, bf16[256,256]{1,0:T(8,128)(2,1)S(1)}, u32[]{:S(2)}, u32[]{:S(2)}) collective-permute-start(bf16[256,256]{1,0:T(8,128)(2,1)S(1)} %shard_map.112.mine_ref), channel_id=1, source_target_pairs={{0,4},{4,0},{1,5},{5,1},{2,6},{6,2},{3,7},{7,3},{8,12},{12,8},{9,1... | collective-permute-start | bytes 393224 | tf_op jit(solution)/shard_map/ppermute | solution.py:30
  59.0 0.7 copy-start.6
  94.3 1.9 %copy-start.3 = (bf16[16,192,512]{2,1,0:T(8,128)(2,1)S(1)}, bf16[16,192,512]{2,1,0:T(8,128)(2,1)}, u32[]{:S(2)}) copy-start(bf16[16,192,512]{2,1,0:T(8,128)(2,1)} %get-tuple-element.29) | copy-start | bytes 9437188
  99.0 19.2 %copy-start.1 = (bf16[3072,512]{1,0:T(8,128)(2,1)}, bf16[3072,512]{1,0:T(8,128)(2,1)S(1)}, u32[]{:S(2)}) copy-start(bf16[3072,512]{1,0:T(8,128)(2,1)S(1)} %get-tuple-element.33.dscore_ref) | copy-start | bytes 9437188
  119.1 21.7 %all-to-all-start.5 = ((f32[16,24,128]{2,1,0:T(8,128)}), f32[16,24,128]{2,1,0:T(8,128)S(1)}, u32[]{:S(2)}, u32[]{:S(2)}) async-start(f32[16,24,128]{2,1,0:T(8,128)} %shard_map.117), calls=%async_computation.5 | async-start | bytes 393216 | tf_op jit(solution)/shard_map/all_to_all | solution.py:34
  127.2 1.9 %copy-start.2 = (bf16[3072,512]{1,0:T(8,128)(2,1)S(1)}, bf16[3072,512]{1,0:T(8,128)(2,1)}, u32[]{:S(2)}) copy-start(bf16[3072,512]{1,0:T(8,128)(2,1)} %copy-done.1) | copy-start | bytes 9437188
  130.1 14.7 %copy-start.7 = (f32[256,256]{1,0:T(8,128)S(1)}, f32[256,256]{1,0:T(8,128)}, u32[]{:S(2)}) copy-start(f32[256,256]{1,0:T(8,128)} %param.13) | copy-start | bytes 786436
  130.1 14.7 %copy-start.8 = (f32[256,256]{1,0:T(8,128)S(1)}, f32[256,256]{1,0:T(8,128)}, u32[]{:S(2)}) copy-start(f32[256,256]{1,0:T(8,128)} %param.11) | copy-start | bytes 786436
  130.1 14.7 %copy-start.9 = (f32[256,256]{1,0:T(8,128)S(1)}, f32[256,256]{1,0:T(8,128)}, u32[]{:S(2)}) copy-start(f32[256,256]{1,0:T(8,128)} %param.12) | copy-start | bytes 786436
  130.2 3.6 %collective-permute-start.2 = (f32[256,256]{1,0:T(8,128)S(1)}, f32[256,256]{1,0:T(8,128)S(1)}, u32[]{:S(2)}, u32[]{:S(2)}) collective-permute-start(f32[256,256]{1,0:T(8,128)S(1)} %get-tuple-element.34), channel_id=1, source_target_pairs={{0,4},{4,0},{1,5},{5,1},{2,6},{6,2},{3,7},{7,3},{8,12},{12,8},{9,1... | collective-permute-start | bytes 786440 | tf_op jit(solution)/shard_map/ppermute | solution.py:30
  141.4 8.8 %all-to-all-start.6 = ((f32[4,24,128]{2,1,0:T(8,128)}), f32[4,24,128]{2,1,0:T(8,128)S(1)}, u32[]{:S(2)}, u32[]{:S(2)}) async-start(f32[4,24,128]{2,1,0:T(8,128)} %shard_map.119), calls=%async_computation.6 | async-start | bytes 98304 | tf_op jit(solution)/shard_map/all_to_all | solution.py:34
  144.7 5.5 %copy-start.5 = (bf16[1,48,256]{2,1,0:T(8,128)(2,1)S(1)}, bf16[1,48,256]{2,1,0:T(8,128)(2,1)}, u32[]{:S(2)}) copy-start(bf16[1,48,256]{2,1,0:T(8,128)(2,1)} %features_ref.3) | copy-start | bytes 73732

commit v2 on v1

--- a/solution.py
+++ b/solution.py
@@ -343,7 +343,7 @@
         scalars=1,
     )
     unit_z = exchanged(unit_z, "z")
-    unit_z, vectors, own_targets = lax.optimization_barrier((unit_z, vectors, targets))
+    unit_z, own_targets = lax.optimization_barrier((unit_z, targets))
     own_direction = small_call(direction_kernel, vectors.shape, jnp.bfloat16, vectors)
     other_direction = swapped(own_direction)
     picked, target_sums = picked_sums(

time: 153 us -> 153 us (level)
  no operation moved by 1% of the time
where the time goes in v2:
time: 153 us; the launch traced here: 151 us
  blocking collectives  51.5 us (34%)
  starting transfers between devices  40 us (26%)
  waiting for transfers between devices  35.9 us (23%)
  Pallas kernels  15.9 us (10%)
  local copies, waits for them, and re-layouts  5.26 us (3%)
  other arithmetic  1.62 us (1%)
    all_to_all x3, blocking collectives, exchanged(): return lax.all_to_all(blocks, axes, 0, 0, tiled=True)  51.5 us
    all_to_all x4, waiting for transfers between devices, exchanged(): return lax.all_to_all(blocks, axes, 0, 0, tiled=True)  34.5 us
    all_to_all x4, starting transfers between devices, exchanged(): return lax.all_to_all(blocks, axes, 0, 0, tiled=True)  34.1 us
    pallas_call x10, Pallas kernels, plain_call(): pl.pallas_call(kernel, in_specs=specs, out_specs=[pl.BlockSpec(memory_spa...  10.7 us
    ppermute x3, starting transfers between devices, swapped(): return lax.ppermute(shard, 'crop', [(0, 1), (1, 0)])  5.9 us
    unnamed x20, local copies, waits for them, and re-layouts  5.26 us
    pallas_call x1, Pallas kernels, picked_sums(): pl.pallas_call(functools.partial(picked_kernel, nz), grid_spec=pltpu.Pref...  5.21 us
  transfers between devices with their start and end apart: 7, of which 5 were waited for; matrix products, arithmetic and copies ran while one was open for 1% of the time, Pallas kernels for 5%

profile of v2, /device:TPU:6, one launch (start us, length us, event | category | flops | bytes accessed | tf_op | source)
XLA Modules:
  0.0 151.0 jit_solution(12240349392376847611)
XLA Ops:
  2.1 15.2 %all-to-all-start = ((bf16[16,24,128]{2,1,0:T(8,128)(2,1)}), bf16[16,24,128]{2,1,0:T(8,128)(2,1)S(1)}, u32[]{:S(2)}, u32[]{:S(2)}) async-start(bf16[16,24,128]{2,1,0:T(8,128)(2,1)} %shard_map.110), calls=%async_computation | async-start | bytes 196608 | tf_op jit(solution)/shard_map/all_to_all | solution.py:34
  17.3 1.9 %collective-permute-start.1 = (bf16[1536,512]{1,0:T(8,128)(2,1)}, bf16[1536,512]{1,0:T(8,128)(2,1)}, u32[]{:S(2)}, u32[]{:S(2)}) collective-permute-start(bf16[1536,512]{1,0:T(8,128)(2,1)} %param.8), channel_id=1, source_target_pairs={{0,4},{4,0},{1,5},{5,1},{2,6},{6,2},{3,7},{7,3},{8,12},{12,8},{9,1... | collective-permute-start | bytes 4718600 | tf_op jit(solution)/shard_map/ppermute | solution.py:30
  19.3 11.6 %all-to-all-done.unit_ref = bf16[16,24,128]{2,1,0:T(8,128)(2,1)S(1)} async-done(((bf16[16,24,128]{2,1,0:T(8,128)(2,1)}), bf16[16,24,128]{2,1,0:T(8,128)(2,1)S(1)}, u32[]{:S(2)}, u32[]{:S(2)}) %all-to-all-start) | async-done | bytes 98336 | tf_op jit(solution)/shard_map/all_to_all | solution.py:34
  30.9 1.3 shard_map.111
  32.2 7.6 %all-to-all-start.1 = ((bf16[16,192,256]{2,1,0:T(8,128)(2,1)}), bf16[16,192,256]{2,1,0:T(8,128)(2,1)S(1)}, u32[]{:S(2)}, u32[]{:S(2)}) async-start(bf16[16,192,256]{2,1,0:T(8,128)(2,1)} %shard_map.111), calls=%async_computation.1 | async-start | bytes 3145728 | tf_op jit(solution)/shard_map/all_to_all | solution.py:34
  39.9 1.9 %collective-permute-start = (bf16[256,256]{1,0:T(8,128)(2,1)S(1)}, bf16[256,256]{1,0:T(8,128)(2,1)S(1)}, u32[]{:S(2)}, u32[]{:S(2)}) collective-permute-start(bf16[256,256]{1,0:T(8,128)(2,1)S(1)} %shard_map.112.mine_ref), channel_id=1, source_target_pairs={{0,4},{4,0},{1,5},{5,1},{2,6},{6,2},{3,7},{7,3},{8,12},{12,8},{9,1... | collective-permute-start | bytes 393224 | tf_op jit(solution)/shard_map/ppermute | solution.py:30
  41.9 5.2 %shard_map.113 = (bf16[16,192,512]{2,1,0:T(8,128)(2,1)}, f32[4,6,128]{2,1,0:T(8,128)}) custom-call(s32[192]{0:T(256)} %bitcast.13, s32[1]{0:T(128)} %bitcast.core_ref, bf16[96,16,512]{2,1,0:T(8,128)(2,1)} %bitcast.12, bf16[96,16,512]{2,1,0:T(8,128)(2,1)} %bitcast.5.other_ref), custom_call_target="tpu_custom_call" | custom-call | tf_op jit(solution)/shard_map/pallas_call | solution.py:121
  47.1 11.9 %all-to-all-done.1 = bf16[16,192,256]{2,1,0:T(8,128)(2,1)S(1)} async-done(((bf16[16,192,256]{2,1,0:T(8,128)(2,1)}), bf16[16,192,256]{2,1,0:T(8,128)(2,1)S(1)}, u32[]{:S(2)}, u32[]{:S(2)}) %all-to-all-start.1) | async-done | bytes 1572896 | tf_op jit(solution)/shard_map/all_to_all | solution.py:34
  59.7 2.2 %shard_map.114 = (bf16[16,48,128]{2,1,0:T(8,128)(2,1)S(1)}, bf16[512,256]{1,0:T(8,128)(2,1)S(1)}, f32[3072,512]{1,0:T(8,128)S(1)}) custom-call(s32[1]{0:T(128)} %bitcast.core_ref, bf16[3072,256]{1,0:T(8,128)(2,1)S(1)} %bitcast.8, bf16[256,256]{1,0:T(8,128)(2,1)S(1)} %shard_map.112.mine_ref, bf16[256,256]{1,0:T(8,128)(2,1)S(1)} %collective-permute-done.theirs_ref, ...), custom_call_target="tpu_custom_call" | custom-call | tf_op jit(solution)/shard_map/pallas_call | solution.py:157
  61.9 20.3 %all_to_all.35.in_ref = bf16[16,48,128]{2,1,0:T(8,128)(2,1)S(1)} all-to-all(bf16[16,48,128]{2,1,0:T(8,128)(2,1)S(1)} %get-tuple-element.24), channel_id=1, replica_groups=mesh['z'=16,'x'=4,'crop'=2,'y'=4] {'z'}, dimensions={0} | all-to-all | bytes 393216 | tf_op jit(solution)/shard_map/all_to_all | solution.py:34
  82.3 12.0 %all_to_all.36.totals_ref = bf16[16,48,128]{2,1,0:T(8,128)(2,1)S(1)} all-to-all(bf16[16,48,128]{2,1,0:T(8,128)(2,1)S(1)} %shard_map.115), channel_id=1, replica_groups=mesh['z'=16,'x'=4,'crop'=2,'y'=4] {'x','y'}, dimensions={0} | all-to-all | bytes 393216 | tf_op jit(solution)/shard_map/all_to_all | solution.py:34
  94.3 1.9 %copy-done.3 = bf16[16,192,512]{2,1,0:T(8,128)(2,1)S(1)} copy-done((bf16[16,192,512]{2,1,0:T(8,128)(2,1)S(1)}, bf16[16,192,512]{2,1,0:T(8,128)(2,1)}, u32[]{:S(2)}) %copy-start.3) | copy-done | bytes 3145752
  96.2 2.8 %shard_map.116 = (bf16[3072,256]{1,0:T(8,128)(2,1)S(1)}, bf16[3072,512]{1,0:T(8,128)(2,1)S(1)}) custom-call(bf16[16,48,128]{2,1,0:T(8,128)(2,1)S(1)} %all_to_all.36.totals_ref, f32[3072,512]{1,0:T(8,128)S(1)} %get-tuple-element.25.expo_ref, bf16[512,256]{1,0:T(8,128)(2,1)S(1)} %get-tuple-element.26.direction_ref, bf16[3072,512]{1,0:T(8,128)(2,1)S(1)} %bitcast.10), custom_call_target="tpu_custom_call" | custom-call | tf_op jit(solution)/shard_map/pallas_call | solution.py:157
  99.0 19.2 %all_to_all.37.in_ref = bf16[16,192,256]{2,1,0:T(8,128)(2,1)S(1)} all-to-all(bf16[16,192,256]{2,1,0:T(8,128)(2,1)S(1)} %bitcast.11), channel_id=1, replica_groups=mesh['z'=16,'x'=4,'crop'=2,'y'=4] {'x','y'}, dimensions={0} | all-to-all | bytes 3145728 | tf_op jit(solution)/shard_map/all_to_all | solution.py:34
  118.2 0.9 shard_map.117
  119.1 8.1 %all-to-all-start.5 = ((f32[16,24,128]{2,1,0:T(8,128)}), f32[16,24,128]{2,1,0:T(8,128)S(1)}, u32[]{:S(2)}, u32[]{:S(2)}) async-start(f32[16,24,128]{2,1,0:T(8,128)} %shard_map.117), calls=%async_computation.5 | async-start | bytes 393216 | tf_op jit(solution)/shard_map/all_to_all | solution.py:34
  127.2 1.9 %copy-done.2 = bf16[3072,512]{1,0:T(8,128)(2,1)S(1)} copy-done((bf16[3072,512]{1,0:T(8,128)(2,1)S(1)}, bf16[3072,512]{1,0:T(8,128)(2,1)}, u32[]{:S(2)}) %copy-start.2) | copy-done | bytes 3145752
  129.1 1.0 shard_map.118
  130.2 2.1 %collective-permute-start.2 = (f32[256,256]{1,0:T(8,128)S(1)}, f32[256,256]{1,0:T(8,128)S(1)}, u32[]{:S(2)}, u32[]{:S(2)}) collective-permute-start(f32[256,256]{1,0:T(8,128)S(1)} %get-tuple-element.32), channel_id=1, source_target_pairs={{0,4},{4,0},{1,5},{5,1},{2,6},{6,2},{3,7},{7,3},{8,12},{12,8},{9,1... | collective-permute-start | bytes 786440 | tf_op jit(solution)/shard_map/ppermute | solution.py:30
  132.3 1.4 collective-permute-done.2
  133.7 7.0 %all-to-all-done.5.in_ref = f32[16,24,128]{2,1,0:T(8,128)S(1)} async-done(((f32[16,24,128]{2,1,0:T(8,128)}), f32[16,24,128]{2,1,0:T(8,128)S(1)}, u32[]{:S(2)}, u32[]{:S(2)}) %all-to-all-start.5) | async-done | bytes 196640 | tf_op jit(solution)/shard_map/all_to_all | solution.py:34
  141.4 3.3 %all-to-all-start.6 = ((f32[4,24,128]{2,1,0:T(8,128)}), f32[4,24,128]{2,1,0:T(8,128)S(1)}, u32[]{:S(2)}, u32[]{:S(2)}) async-start(f32[4,24,128]{2,1,0:T(8,128)} %shard_map.119), calls=%async_computation.6 | async-start | bytes 98304 | tf_op jit(solution)/shard_map/all_to_all | solution.py:34
  144.9 1.3 multiply_add_fusion
  146.2 4.0 %all-to-all-done.6.dunit_ref = f32[4,24,128]{2,1,0:T(8,128)S(1)} async-done(((f32[4,24,128]{2,1,0:T(8,128)}), f32[4,24,128]{2,1,0:T(8,128)S(1)}, u32[]{:S(2)}, u32[]{:S(2)}) %all-to-all-start.6) | async-done | bytes 49184 | tf_op jit(solution)/shard_map/all_to_all | solution.py:34
  (28 shorter events, 4.2 us)
Async XLA Ops:
  0.6 0.7 copy-start.4
  2.1 28.8 %all-to-all-start = ((bf16[16,24,128]{2,1,0:T(8,128)(2,1)}), bf16[16,24,128]{2,1,0:T(8,128)(2,1)S(1)}, u32[]{:S(2)}, u32[]{:S(2)}) async-start(bf16[16,24,128]{2,1,0:T(8,128)(2,1)} %shard_map.110), calls=%async_computation | async-start | bytes 196608 | tf_op jit(solution)/shard_map/all_to_all | solution.py:34
  17.3 24.5 %collective-permute-start.1 = (bf16[1536,512]{1,0:T(8,128)(2,1)}, bf16[1536,512]{1,0:T(8,128)(2,1)}, u32[]{:S(2)}, u32[]{:S(2)}) collective-permute-start(bf16[1536,512]{1,0:T(8,128)(2,1)} %param.8), channel_id=1, source_target_pairs={{0,4},{4,0},{1,5},{5,1},{2,6},{6,2},{3,7},{7,3},{8,12},{12,8},{9,1... | collective-permute-start | bytes 4718600 | tf_op jit(solution)/shard_map/ppermute | solution.py:30
  32.2 7.6 %copy-start = (f32[256,256]{1,0:T(8,128)S(1)}, f32[256,256]{1,0:T(8,128)}, u32[]{:S(2)}) copy-start(f32[256,256]{1,0:T(8,128)} %vectors_ref.1) | copy-start | bytes 786436
  32.2 26.8 %all-to-all-start.1 = ((bf16[16,192,256]{2,1,0:T(8,128)(2,1)}), bf16[16,192,256]{2,1,0:T(8,128)(2,1)S(1)}, u32[]{:S(2)}, u32[]{:S(2)}) async-start(bf16[16,192,256]{2,1,0:T(8,128)(2,1)} %shard_map.111), calls=%async_computation.1 | async-start | bytes 3145728 | tf_op jit(solution)/shard_map/all_to_all | solution.py:34
  39.9 7.2 %collective-permute-start = (bf16[256,256]{1,0:T(8,128)(2,1)S(1)}, bf16[256,256]{1,0:T(8,128)(2,1)S(1)}, u32[]{:S(2)}, u32[]{:S(2)}) collective-permute-start(bf16[256,256]{1,0:T(8,128)(2,1)S(1)} %shard_map.112.mine_ref), channel_id=1, source_target_pairs={{0,4},{4,0},{1,5},{5,1},{2,6},{6,2},{3,7},{7,3},{8,12},{12,8},{9,1... | collective-permute-start | bytes 393224 | tf_op jit(solution)/shard_map/ppermute | solution.py:30
  59.0 0.7 copy-start.6
  94.3 1.9 %copy-start.3 = (bf16[16,192,512]{2,1,0:T(8,128)(2,1)S(1)}, bf16[16,192,512]{2,1,0:T(8,128)(2,1)}, u32[]{:S(2)}) copy-start(bf16[16,192,512]{2,1,0:T(8,128)(2,1)} %get-tuple-element.27) | copy-start | bytes 9437188
  99.0 19.2 %copy-start.1 = (bf16[3072,512]{1,0:T(8,128)(2,1)}, bf16[3072,512]{1,0:T(8,128)(2,1)S(1)}, u32[]{:S(2)}) copy-start(bf16[3072,512]{1,0:T(8,128)(2,1)S(1)} %get-tuple-element.31.dscore_ref) | copy-start | bytes 9437188
  119.1 21.7 %all-to-all-start.5 = ((f32[16,24,128]{2,1,0:T(8,128)}), f32[16,24,128]{2,1,0:T(8,128)S(1)}, u32[]{:S(2)}, u32[]{:S(2)}) async-start(f32[16,24,128]{2,1,0:T(8,128)} %shard_map.117), calls=%async_computation.5 | async-start | bytes 393216 | tf_op jit(solution)/shard_map/all_to_all | solution.py:34
  127.2 1.9 %copy-start.2 = (bf16[3072,512]{1,0:T(8,128)(2,1)S(1)}, bf16[3072,512]{1,0:T(8,128)(2,1)}, u32[]{:S(2)}) copy-start(bf16[3072,512]{1,0:T(8,128)(2,1)} %copy-done.1) | copy-start | bytes 9437188
  130.1 14.7 %copy-start.7 = (f32[256,256]{1,0:T(8,128)S(1)}, f32[256,256]{1,0:T(8,128)}, u32[]{:S(2)}) copy-start(f32[256,256]{1,0:T(8,128)} %param.13) | copy-start | bytes 786436
  130.1 14.7 %copy-start.8 = (f32[256,256]{1,0:T(8,128)S(1)}, f32[256,256]{1,0:T(8,128)}, u32[]{:S(2)}) copy-start(f32[256,256]{1,0:T(8,128)} %param.11) | copy-start | bytes 786436
  130.1 14.7 %copy-start.9 = (f32[256,256]{1,0:T(8,128)S(1)}, f32[256,256]{1,0:T(8,128)}, u32[]{:S(2)}) copy-start(f32[256,256]{1,0:T(8,128)} %param.12) | copy-start | bytes 786436
  130.2 3.6 %collective-permute-start.2 = (f32[256,256]{1,0:T(8,128)S(1)}, f32[256,256]{1,0:T(8,128)S(1)}, u32[]{:S(2)}, u32[]{:S(2)}) collective-permute-start(f32[256,256]{1,0:T(8,128)S(1)} %get-tuple-element.32), channel_id=1, source_target_pairs={{0,4},{4,0},{1,5},{5,1},{2,6},{6,2},{3,7},{7,3},{8,12},{12,8},{9,1... | collective-permute-start | bytes 786440 | tf_op jit(solution)/shard_map/ppermute | solution.py:30
  141.4 8.8 %all-to-all-start.6 = ((f32[4,24,128]{2,1,0:T(8,128)}), f32[4,24,128]{2,1,0:T(8,128)S(1)}, u32[]{:S(2)}, u32[]{:S(2)}) async-start(f32[4,24,128]{2,1,0:T(8,128)} %shard_map.119), calls=%async_computation.6 | async-start | bytes 98304 | tf_op jit(solution)/shard_map/all_to_all | solution.py:34
  144.7 5.5 %copy-start.5 = (bf16[1,48,256]{2,1,0:T(8,128)(2,1)S(1)}, bf16[1,48,256]{2,1,0:T(8,128)(2,1)}, u32[]{:S(2)}) copy-start(bf16[1,48,256]{2,1,0:T(8,128)(2,1)} %features_ref.3) | copy-start | bytes 73732
